TPU v7x, 32 devices: a whole 2x2x4 slice. The times are simulated.
32 devices in a mesh: rows: 32 (over z, y, x, core).
Axes of the slice: x: 2, y: 2, z: 4, core: 2. Of those that a mesh axis runs over, the one named last changes fastest.
Arguments:
- ham: bfloat16 [32, 10, 128, 128], P('rows'), may hold values from -0.5 to 0.5
- hpat: int32 [32, 10], replicated, may hold values from -1 to 31, as said below
- kpat: int32 [32, 30], replicated, may hold values from -1 to 31, as said below
- coefs: float32 [4], replicated, may hold values from -1 to 1
Outputs:
- density: float32 [32, 30, 128, 128], P('rows')
Inputs may be any that keep to these rules, and one draw needn't show every extreme that they name: Slot 0 of row i of hpat is i; the used slots of a row name distinct block columns within 6 of i; unused slots (-1) occur only where fewer than 10 columns lie inside the grid. Slot 0 of row i of kpat is i; the used slots of a row name distinct block columns within 24 of i, from half of 30 to 30 of them (fewer only near the grid's ends); some row uses all 30 slots; unused slots hold -1.
All inputs are finite; a program needn't handle non-finite values.
Results may differ from a plain program's by a relative error of at most 0.0029.
Values may be sent and summed in bfloat16 or wider, within the bound.
A program may use at most 128 MiB of HBM per device.

v0:
```python
import jax
import jax.numpy as jnp
from jax import lax
from jax.sharding import PartitionSpec as P

HREACH = 6


def from_behind(x, axis, by):
    peers = lax.axis_size(axis)
    pairs = [(i, i + by) for i in range(peers) if 0 <= i + by < peers]
    return lax.ppermute(x, axis, pairs)


def body(ham, hpat, kpat, coefs):
    own = lax.axis_index("rows")
    count = lax.axis_size("rows")
    row_h = lax.dynamic_index_in_dim(hpat, own, 0, keepdims=False)
    row_k = lax.dynamic_index_in_dim(kpat, own, 0, keepdims=False)
    local = ham[0]
    blk = local.shape[-1]
    eye = jnp.eye(blk, dtype=jnp.float32)
    term0 = jnp.where(
        (row_k == own)[:, None, None], eye[None], jnp.zeros((1, blk, blk), jnp.float32)
    )
    match_one = ((row_h[None, :] == row_k[:, None]) & (row_k[:, None] >= 0)).astype(jnp.float32)
    term1 = jnp.einsum(
        "jh,hab->jab", match_one, local.astype(jnp.float32), precision=lax.Precision.HIGHEST
    )

    def select(blocks, pattern, offset):
        owner = own + offset
        hit = row_h == owner
        used = jnp.any(hit)
        which = jnp.argmax(hit)
        left = lax.dynamic_index_in_dim(local, which, 0, keepdims=False)
        left = jnp.where(used, left, jnp.zeros_like(left))
        pats = lax.dynamic_index_in_dim(pattern, jnp.clip(owner, 0, count - 1), 0, keepdims=False)
        match = (pats[None, :] == row_k[:, None]) & (row_k[:, None] >= 0)
        slot = jnp.argmax(match, axis=1)
        found = jnp.any(match, axis=1)
        picked = jnp.take(blocks, slot, axis=0)
        picked = jnp.where(found[:, None, None], picked, jnp.zeros_like(picked))
        return (left, picked)

    def combine(selected):
        lefts = jnp.stack([pair[0] for pair in selected], axis=0)
        pickeds = jnp.stack([pair[1] for pair in selected], axis=0)
        return jnp.einsum("dab,djbc->jac", lefts, pickeds, preferred_element_type=jnp.float32)

    distances = [step for step in range(-HREACH, HREACH + 1) if step != 0]
    chosen = [select(local, hpat, 0)]
    for step in distances:
        fetched = from_behind(ham, "rows", -step)
        chosen.append(select(fetched[0], hpat, step))
    second = combine(chosen)
    term2 = (2.0 * second - term0).astype(jnp.bfloat16)
    stacked = term2[None]
    chosen_term = [select(term2, kpat, 0)]
    for step in distances:
        fetched_term = from_behind(stacked, "rows", -step)
        chosen_term.append(select(fetched_term[0], kpat, step))
    third = combine(chosen_term)
    term3 = 2.0 * third - term1
    density = (
        coefs[0] * term0
        + coefs[1] * term1
        + coefs[2] * term2.astype(jnp.float32)
        + coefs[3] * term3
    )
    return density[None]


def solution(mesh):
    in_specs = (P("rows", None, None, None), P(), P(), P())
    out_specs = P("rows", None, None, None)
    return jax.shard_map(body, mesh=mesh, in_specs=in_specs, out_specs=out_specs, check_vma=False)
```

profile of v0, /device:TPU:18, one launch (start us, length us, event | category | flops | bytes accessed | tf_op | source)
XLA Modules:
  0.0 504.1 jit_solution(3479249233164375845)
XLA Ops:
  0.0 3.4 collective-permute-start
  8.8 3.2 collective-permute-start.3
  12.0 3.0 collective-permute-start.4
  103.3 3.6 collective-permute-start.6
  107.4 4.6 collective-permute-start.7
  114.0 3.3 collective-permute-start.9
  117.3 5.4 %collective-permute-start.10 = (bf16[1,10,128,128]{3,2,1,0:T(8,128)(2,1)}, bf16[1,10,128,128]{3,2,1,0:T(8,128)(2,1)}, u32[]{:S(2)}, u32[]{:S(2)}) collective-permute-start(bf16[1,10,128,128]{3,2,1,0:T(8,128)(2,1)} %param.8), channel_id=1, source_target_pairs={{5,0},{6,1},{7,2},{8,3},{9,4},{10,5},{11,6},{12,7},{13,8},{14,9},{... | collective-permute-start | bytes 983048 | tf_op jit(solution)/shard_map/ppermute | solution.py:12
  200.8 8.1 %fusion.4 = bf16[30,128,128]{1,2,0:T(8,128)(2,1)S(1)} fusion(bf16[13,30,128,128]{2,3,0,1:T(8,128)(2,1)} %bitcast_dynamic-update-slice_fusion.25, f32[128,128]{0,1:T(8,128)S(1)} %fusion.10, pred[30]{0:T(512)(128)(4,1)S(1)} %copy-done.58, bf16[13,128,128]{2,1,0:T(8,128)(2,1)S(1)} %copy-done.22), kind=kOutput, calls=%fused_computation.32 | convolution fusion | flops 1637744640 | bytes 14254110 | tf_op jit(solution)/shard_map/dab,djbc->jac/dot_general | solution.py:49
  210.2 4.8 collective-permute-start.12
  218.7 4.1 collective-permute-start.14
  227.2 11.9 %collective-permute-done.12 = bf16[1,30,128,128]{3,2,1,0:T(8,128)(2,1)S(1)} collective-permute-done((bf16[1,30,128,128]{3,2,1,0:T(8,128)(2,1)}, bf16[1,30,128,128]{3,2,1,0:T(8,128)(2,1)S(1)}, u32[]{:S(2)}, u32[]{:S(2)}) %collective-permute-start.12) | collective-permute-done | bytes 983072 | tf_op jit(solution)/shard_map/ppermute | solution.py:12
  241.0 26.5 %collective-permute-done.13 = bf16[1,30,128,128]{3,2,1,0:T(8,128)(2,1)S(1)} collective-permute-done((bf16[1,30,128,128]{3,2,1,0:T(8,128)(2,1)}, bf16[1,30,128,128]{3,2,1,0:T(8,128)(2,1)S(1)}, u32[]{:S(2)}, u32[]{:S(2)}) %collective-permute-start.13) | collective-permute-done | bytes 983072 | tf_op jit(solution)/shard_map/ppermute | solution.py:12
  271.2 49.1 %collective-permute-done.14 = bf16[1,30,128,128]{3,2,1,0:T(8,128)(2,1)} collective-permute-done((bf16[1,30,128,128]{3,2,1,0:T(8,128)(2,1)}, bf16[1,30,128,128]{3,2,1,0:T(8,128)(2,1)}, u32[]{:S(2)}, u32[]{:S(2)}) %collective-permute-start.14) | collective-permute-done | bytes 983072 | tf_op jit(solution)/shard_map/ppermute | solution.py:12
  328.0 7.5 %collective-permute-start.23 = (bf16[1,30,128,128]{3,2,1,0:T(8,128)(2,1)}, bf16[1,30,128,128]{3,2,1,0:T(8,128)(2,1)}, u32[]{:S(2)}, u32[]{:S(2)}) collective-permute-start(bf16[1,30,128,128]{3,2,1,0:T(8,128)(2,1)} %copy.206), channel_id=1, source_target_pairs={{6,0},{7,1},{8,2},{9,3},{10,4},{11,5},{12,6},{13,7},{14,8},{15,9},... | collective-permute-start | bytes 2949128 | tf_op jit(solution)/shard_map/ppermute | solution.py:12
  347.7 2.9 gather_fusion.15
  352.2 2.9 gather_fusion.16
  356.7 2.9 gather_fusion.17
  361.9 2.9 gather_fusion.18
  367.1 2.9 gather_fusion.19
  372.3 2.9 gather_fusion.20
  378.3 2.9 gather_fusion.21
  395.1 9.8 %collective-permute-done.22 = bf16[1,30,128,128]{3,2,1,0:T(8,128)(2,1)} collective-permute-done((bf16[1,30,128,128]{3,2,1,0:T(8,128)(2,1)}, bf16[1,30,128,128]{3,2,1,0:T(8,128)(2,1)}, u32[]{:S(2)}, u32[]{:S(2)}) %collective-permute-start.22) | collective-permute-done | bytes 983072 | tf_op jit(solution)/shard_map/ppermute | solution.py:12
  410.0 57.0 %collective-permute-done.23 = bf16[1,30,128,128]{3,2,1,0:T(8,128)(2,1)} collective-permute-done((bf16[1,30,128,128]{3,2,1,0:T(8,128)(2,1)}, bf16[1,30,128,128]{3,2,1,0:T(8,128)(2,1)}, u32[]{:S(2)}, u32[]{:S(2)}) %collective-permute-start.23) | collective-permute-done | bytes 983072 | tf_op jit(solution)/shard_map/ppermute | solution.py:12
  492.9 9.3 %fusion.3 = f32[1,30,128,128]{2,3,1,0:T(8,128)S(1)} fusion(f32[30,128,128]{1,2,0:T(8,128)S(1)} %copy-done.18, bf16[30,128,128]{1,2,0:T(8,128)(2,1)S(1)} %copy-done.12, bf16[13,30,128,128]{2,3,1,0:T(8,128)(2,1)} %bitcast_dynamic-update-slice_fusion.12, f32[]{:T(128)} %bitcast.60, f32[]{:T(128)} %bitcast.5, f32[]{:T(128)} %bitcast.2, ...), kind=kOutput, calls=%fused_computation.31 | convolution fusion | flops 1641185280 | bytes 18186286 | tf_op jit(solution)/shard_map/dab,djbc->jac/dot_general | solution.py:49
  (390 shorter events, 244.2 us)
Async XLA Ops:
  0.0 101.3 %collective-permute-start = (bf16[1,10,128,128]{3,2,1,0:T(8,128)(2,1)}, bf16[1,10,128,128]{3,2,1,0:T(8,128)(2,1)S(1)}, u32[]{:S(2)}, u32[]{:S(2)}) collective-permute-start(bf16[1,10,128,128]{3,2,1,0:T(8,128)(2,1)} %param.8), channel_id=1, source_target_pairs={{0,6},{1,7},{2,8},{3,9},{4,10},{5,11},{6,12},{7,13},{8,14},{9,15},... | collective-permute-start | bytes 983048 | tf_op jit(solution)/shard_map/ppermute | solution.py:12
  3.5 99.8 %collective-permute-start.1 = (bf16[1,10,128,128]{3,2,1,0:T(8,128)(2,1)}, bf16[1,10,128,128]{3,2,1,0:T(8,128)(2,1)S(1)}, u32[]{:S(2)}, u32[]{:S(2)}) collective-permute-start(bf16[1,10,128,128]{3,2,1,0:T(8,128)(2,1)} %param.8), channel_id=1, source_target_pairs={{0,5},{1,6},{2,7},{3,8},{4,9},{5,10},{6,11},{7,12},{8,13},{9,14},{... | collective-permute-start | bytes 983048 | tf_op jit(solution)/shard_map/ppermute | solution.py:12
  6.1 101.4 %collective-permute-start.2 = (bf16[1,10,128,128]{3,2,1,0:T(8,128)(2,1)}, bf16[1,10,128,128]{3,2,1,0:T(8,128)(2,1)S(1)}, u32[]{:S(2)}, u32[]{:S(2)}) collective-permute-start(bf16[1,10,128,128]{3,2,1,0:T(8,128)(2,1)} %param.8), channel_id=1, source_target_pairs={{0,4},{1,5},{2,6},{3,7},{4,8},{5,9},{6,10},{7,11},{8,12},{9,13},{1... | collective-permute-start | bytes 983048 | tf_op jit(solution)/shard_map/ppermute | solution.py:12
  8.8 103.2 %collective-permute-start.3 = (bf16[1,10,128,128]{3,2,1,0:T(8,128)(2,1)}, bf16[1,10,128,128]{3,2,1,0:T(8,128)(2,1)S(1)}, u32[]{:S(2)}, u32[]{:S(2)}) collective-permute-start(bf16[1,10,128,128]{3,2,1,0:T(8,128)(2,1)} %param.8), channel_id=1, source_target_pairs={{0,3},{1,4},{2,5},{3,6},{4,7},{5,8},{6,9},{7,10},{8,11},{9,12},{10... | collective-permute-start | bytes 983048 | tf_op jit(solution)/shard_map/ppermute | solution.py:12
  12.0 102.0 %collective-permute-start.4 = (bf16[1,10,128,128]{3,2,1,0:T(8,128)(2,1)}, bf16[1,10,128,128]{3,2,1,0:T(8,128)(2,1)S(1)}, u32[]{:S(2)}, u32[]{:S(2)}) collective-permute-start(bf16[1,10,128,128]{3,2,1,0:T(8,128)(2,1)} %param.8), channel_id=1, source_target_pairs={{0,2},{1,3},{2,4},{3,5},{4,6},{5,7},{6,8},{7,9},{8,10},{9,11},{10,... | collective-permute-start | bytes 983048 | tf_op jit(solution)/shard_map/ppermute | solution.py:12
  101.3 16.0 %collective-permute-start.5 = (bf16[1,10,128,128]{3,2,1,0:T(8,128)(2,1)}, bf16[1,10,128,128]{3,2,1,0:T(8,128)(2,1)S(1)}, u32[]{:S(2)}, u32[]{:S(2)}) collective-permute-start(bf16[1,10,128,128]{3,2,1,0:T(8,128)(2,1)} %param.8), channel_id=1, source_target_pairs={{0,1},{1,2},{2,3},{3,4},{4,5},{5,6},{6,7},{7,8},{8,9},{9,10},{10,1... | collective-permute-start | bytes 983048 | tf_op jit(solution)/shard_map/ppermute | solution.py:12
  103.3 19.5 %collective-permute-start.6 = (bf16[1,10,128,128]{3,2,1,0:T(8,128)(2,1)}, bf16[1,10,128,128]{3,2,1,0:T(8,128)(2,1)S(1)}, u32[]{:S(2)}, u32[]{:S(2)}) collective-permute-start(bf16[1,10,128,128]{3,2,1,0:T(8,128)(2,1)} %param.8), channel_id=1, source_target_pairs={{1,0},{2,1},{3,2},{4,3},{5,4},{6,5},{7,6},{8,7},{9,8},{10,9},{11,1... | collective-permute-start | bytes 983048 | tf_op jit(solution)/shard_map/ppermute | solution.py:12
  107.4 48.1 %collective-permute-start.7 = (bf16[1,10,128,128]{3,2,1,0:T(8,128)(2,1)}, bf16[1,10,128,128]{3,2,1,0:T(8,128)(2,1)}, u32[]{:S(2)}, u32[]{:S(2)}) collective-permute-start(bf16[1,10,128,128]{3,2,1,0:T(8,128)(2,1)} %param.8), channel_id=1, source_target_pairs={{2,0},{3,1},{4,2},{5,3},{6,4},{7,5},{8,6},{9,7},{10,8},{11,9},{12,... | collective-permute-start | bytes 983048 | tf_op jit(solution)/shard_map/ppermute | solution.py:12
  112.0 48.4 %collective-permute-start.8 = (bf16[1,10,128,128]{3,2,1,0:T(8,128)(2,1)}, bf16[1,10,128,128]{3,2,1,0:T(8,128)(2,1)}, u32[]{:S(2)}, u32[]{:S(2)}) collective-permute-start(bf16[1,10,128,128]{3,2,1,0:T(8,128)(2,1)} %param.8), channel_id=1, source_target_pairs={{3,0},{4,1},{5,2},{6,3},{7,4},{8,5},{9,6},{10,7},{11,8},{12,9},{13... | collective-permute-start | bytes 983048 | tf_op jit(solution)/shard_map/ppermute | solution.py:12
  114.0 51.3 %collective-permute-start.9 = (bf16[1,10,128,128]{3,2,1,0:T(8,128)(2,1)}, bf16[1,10,128,128]{3,2,1,0:T(8,128)(2,1)}, u32[]{:S(2)}, u32[]{:S(2)}) collective-permute-start(bf16[1,10,128,128]{3,2,1,0:T(8,128)(2,1)} %param.8), channel_id=1, source_target_pairs={{4,0},{5,1},{6,2},{7,3},{8,4},{9,5},{10,6},{11,7},{12,8},{13,9},{1... | collective-permute-start | bytes 983048 | tf_op jit(solution)/shard_map/ppermute | solution.py:12
  117.3 52.8 %collective-permute-start.10 = (bf16[1,10,128,128]{3,2,1,0:T(8,128)(2,1)}, bf16[1,10,128,128]{3,2,1,0:T(8,128)(2,1)}, u32[]{:S(2)}, u32[]{:S(2)}) collective-permute-start(bf16[1,10,128,128]{3,2,1,0:T(8,128)(2,1)} %param.8), channel_id=1, source_target_pairs={{5,0},{6,1},{7,2},{8,3},{9,4},{10,5},{11,6},{12,7},{13,8},{14,9},{... | collective-permute-start | bytes 983048 | tf_op jit(solution)/shard_map/ppermute | solution.py:12
  122.8 52.2 %collective-permute-start.11 = (bf16[1,10,128,128]{3,2,1,0:T(8,128)(2,1)}, bf16[1,10,128,128]{3,2,1,0:T(8,128)(2,1)}, u32[]{:S(2)}, u32[]{:S(2)}) collective-permute-start(bf16[1,10,128,128]{3,2,1,0:T(8,128)(2,1)} %param.8), channel_id=1, source_target_pairs={{6,0},{7,1},{8,2},{9,3},{10,4},{11,5},{12,6},{13,7},{14,8},{15,9},... | collective-permute-start | bytes 983048 | tf_op jit(solution)/shard_map/ppermute | solution.py:12
  210.2 28.9 %collective-permute-start.12 = (bf16[1,30,128,128]{3,2,1,0:T(8,128)(2,1)}, bf16[1,30,128,128]{3,2,1,0:T(8,128)(2,1)S(1)}, u32[]{:S(2)}, u32[]{:S(2)}) collective-permute-start(bf16[1,30,128,128]{3,2,1,0:T(8,128)(2,1)} %copy.206), channel_id=1, source_target_pairs={{0,6},{1,7},{2,8},{3,9},{4,10},{5,11},{6,12},{7,13},{8,14},{9,15},... | collective-permute-start | bytes 2949128 | tf_op jit(solution)/shard_map/ppermute | solution.py:12
  215.0 52.5 %collective-permute-start.13 = (bf16[1,30,128,128]{3,2,1,0:T(8,128)(2,1)}, bf16[1,30,128,128]{3,2,1,0:T(8,128)(2,1)S(1)}, u32[]{:S(2)}, u32[]{:S(2)}) collective-permute-start(bf16[1,30,128,128]{3,2,1,0:T(8,128)(2,1)} %copy.206), channel_id=1, source_target_pairs={{0,5},{1,6},{2,7},{3,8},{4,9},{5,10},{6,11},{7,12},{8,13},{9,14},{... | collective-permute-start | bytes 2949128 | tf_op jit(solution)/shard_map/ppermute | solution.py:12
  218.7 101.5 %collective-permute-start.14 = (bf16[1,30,128,128]{3,2,1,0:T(8,128)(2,1)}, bf16[1,30,128,128]{3,2,1,0:T(8,128)(2,1)}, u32[]{:S(2)}, u32[]{:S(2)}) collective-permute-start(bf16[1,30,128,128]{3,2,1,0:T(8,128)(2,1)} %copy.206), channel_id=1, source_target_pairs={{0,4},{1,5},{2,6},{3,7},{4,8},{5,9},{6,10},{7,11},{8,12},{9,13},{1... | collective-permute-start | bytes 2949128 | tf_op jit(solution)/shard_map/ppermute | solution.py:12
  222.8 99.3 %collective-permute-start.15 = (bf16[1,30,128,128]{3,2,1,0:T(8,128)(2,1)}, bf16[1,30,128,128]{3,2,1,0:T(8,128)(2,1)}, u32[]{:S(2)}, u32[]{:S(2)}) collective-permute-start(bf16[1,30,128,128]{3,2,1,0:T(8,128)(2,1)} %copy.206), channel_id=1, source_target_pairs={{0,3},{1,4},{2,5},{3,6},{4,7},{5,8},{6,9},{7,10},{8,11},{9,12},{10... | collective-permute-start | bytes 2949128 | tf_op jit(solution)/shard_map/ppermute | solution.py:12
  224.7 99.4 %collective-permute-start.16 = (bf16[1,30,128,128]{3,2,1,0:T(8,128)(2,1)}, bf16[1,30,128,128]{3,2,1,0:T(8,128)(2,1)}, u32[]{:S(2)}, u32[]{:S(2)}) collective-permute-start(bf16[1,30,128,128]{3,2,1,0:T(8,128)(2,1)} %copy.206), channel_id=1, source_target_pairs={{0,2},{1,3},{2,4},{3,5},{4,6},{5,7},{6,8},{7,9},{8,10},{9,11},{10,... | collective-permute-start | bytes 2949128 | tf_op jit(solution)/shard_map/ppermute | solution.py:12
  239.1 86.9 %collective-permute-start.17 = (bf16[1,30,128,128]{3,2,1,0:T(8,128)(2,1)}, bf16[1,30,128,128]{3,2,1,0:T(8,128)(2,1)}, u32[]{:S(2)}, u32[]{:S(2)}) collective-permute-start(bf16[1,30,128,128]{3,2,1,0:T(8,128)(2,1)} %copy.206), channel_id=1, source_target_pairs={{0,1},{1,2},{2,3},{3,4},{4,5},{5,6},{6,7},{7,8},{8,9},{9,10},{10,1... | collective-permute-start | bytes 2949128 | tf_op jit(solution)/shard_map/ppermute | solution.py:12
  267.5 60.4 %collective-permute-start.18 = (bf16[1,30,128,128]{3,2,1,0:T(8,128)(2,1)}, bf16[1,30,128,128]{3,2,1,0:T(8,128)(2,1)}, u32[]{:S(2)}, u32[]{:S(2)}) collective-permute-start(bf16[1,30,128,128]{3,2,1,0:T(8,128)(2,1)} %copy.206), channel_id=1, source_target_pairs={{1,0},{2,1},{3,2},{4,3},{5,4},{6,5},{7,6},{8,7},{9,8},{10,9},{11,1... | collective-permute-start | bytes 2949128 | tf_op jit(solution)/shard_map/ppermute | solution.py:12
  320.2 58.1 %collective-permute-start.19 = (bf16[1,30,128,128]{3,2,1,0:T(8,128)(2,1)}, bf16[1,30,128,128]{3,2,1,0:T(8,128)(2,1)}, u32[]{:S(2)}, u32[]{:S(2)}) collective-permute-start(bf16[1,30,128,128]{3,2,1,0:T(8,128)(2,1)} %copy.206), channel_id=1, source_target_pairs={{2,0},{3,1},{4,2},{5,3},{6,4},{7,5},{8,6},{9,7},{10,8},{11,9},{12,... | collective-permute-start | bytes 2949128 | tf_op jit(solution)/shard_map/ppermute | solution.py:12
  322.1 61.3 %collective-permute-start.20 = (bf16[1,30,128,128]{3,2,1,0:T(8,128)(2,1)}, bf16[1,30,128,128]{3,2,1,0:T(8,128)(2,1)}, u32[]{:S(2)}, u32[]{:S(2)}) collective-permute-start(bf16[1,30,128,128]{3,2,1,0:T(8,128)(2,1)} %copy.206), channel_id=1, source_target_pairs={{3,0},{4,1},{5,2},{6,3},{7,4},{8,5},{9,6},{10,7},{11,8},{12,9},{13... | collective-permute-start | bytes 2949128 | tf_op jit(solution)/shard_map/ppermute | solution.py:12
  324.1 65.9 %collective-permute-start.21 = (bf16[1,30,128,128]{3,2,1,0:T(8,128)(2,1)}, bf16[1,30,128,128]{3,2,1,0:T(8,128)(2,1)}, u32[]{:S(2)}, u32[]{:S(2)}) collective-permute-start(bf16[1,30,128,128]{3,2,1,0:T(8,128)(2,1)} %copy.206), channel_id=1, source_target_pairs={{4,0},{5,1},{6,2},{7,3},{8,4},{9,5},{10,6},{11,7},{12,8},{13,9},{1... | collective-permute-start | bytes 2949128 | tf_op jit(solution)/shard_map/ppermute | solution.py:12
  326.0 78.9 %collective-permute-start.22 = (bf16[1,30,128,128]{3,2,1,0:T(8,128)(2,1)}, bf16[1,30,128,128]{3,2,1,0:T(8,128)(2,1)}, u32[]{:S(2)}, u32[]{:S(2)}) collective-permute-start(bf16[1,30,128,128]{3,2,1,0:T(8,128)(2,1)} %copy.206), channel_id=1, source_target_pairs={{5,0},{6,1},{7,2},{8,3},{9,4},{10,5},{11,6},{12,7},{13,8},{14,9},{... | collective-permute-start | bytes 2949128 | tf_op jit(solution)/shard_map/ppermute | solution.py:12
  328.0 139.0 %collective-permute-start.23 = (bf16[1,30,128,128]{3,2,1,0:T(8,128)(2,1)}, bf16[1,30,128,128]{3,2,1,0:T(8,128)(2,1)}, u32[]{:S(2)}, u32[]{:S(2)}) collective-permute-start(bf16[1,30,128,128]{3,2,1,0:T(8,128)(2,1)} %copy.206), channel_id=1, source_target_pairs={{6,0},{7,1},{8,2},{9,3},{10,4},{11,5},{12,6},{13,7},{14,8},{15,9},... | collective-permute-start | bytes 2949128 | tf_op jit(solution)/shard_map/ppermute | solution.py:12
  (72 other events, 3353.9 us)
where the time goes:
time: 508 us; the launch traced here: 504 us
  waiting for transfers between devices  157 us (31%)
  local copies, waits for them, and re-layouts  123 us (24%)
  other arithmetic  109 us (21%)
  starting transfers between devices  72 us (14%)
  between operations  24.8 us (5%)
  matrix products  18 us (4%)
    ppermute x24, waiting for transfers between devices, from_behind(): return lax.ppermute(x, axis, pairs)  157 us
    gather x52, local copies, waits for them, and re-layouts, select(): picked = jnp.take(blocks, slot, axis=0)  112 us
    ppermute x24, starting transfers between devices, from_behind(): return lax.ppermute(x, axis, pairs)  72 us
    unnamed x36, other arithmetic  59.5 us
    dot_general x2, matrix products, combine(): jnp.einsum('dab,djbc->jac', lefts, pickeds, preferred_element_type=jnp.fl...  17.5 us
    another operation x26, other arithmetic, select(): slot = jnp.argmax(match, axis=1)  17 us
    and x25, other arithmetic, select(): picked = jnp.take(blocks, slot, axis=0)  15.5 us
  transfers between devices with their start and end apart: 24, of which 7 were waited for; matrix products, arithmetic and copies ran while one was open for 35% of the time, Pallas kernels for 0%

commit v1 on v0

v1 whole, which is shorter than its diff:
```python
import functools

import jax
import jax.numpy as jnp
from jax import lax
from jax.experimental import pallas as pl
from jax.experimental.pallas import tpu as pltpu
from jax.sharding import PartitionSpec as P

R = 6
SPAN = 2 * R + 1
WIDE = 4 * R + 1
COLS = 6 * R + 1
TALL = SPAN + 2
MESH = pl.DeviceIdType.MESH


def kernel(count, coefs, inv, tidx, slot1, diag, ham, out, *scratch):
    w = scratch[:WIDE]
    band, t2, send, fsend, recv = scratch[WIDE:]
    b = ham.shape[-1]
    kb = out.shape[0]
    mid = 2 * R
    me = lax.axis_index("rows")
    delta = 1 - 2 * lax.rem(me, 2)
    sib = me + delta

    def inside(row):
        return (row >= 0) & (row < count)

    barrier = pltpu.get_barrier_semaphore()
    pl.semaphore_signal(barrier, inc=1, device_id=(sib,), device_id_type=MESH)
    steps = [s * sign for s in range(1, R + 1) for sign in (1, -1)]
    for s in steps:
        @pl.when(inside(me + 2 * s))
        def _(s=s):
            pl.semaphore_signal(barrier, inc=1, device_id=(me + 2 * s,), device_id_type=MESH)
    peers = 1 + sum(jnp.where(inside(me + 2 * s), 1, 0) for s in steps)
    pl.semaphore_wait(barrier, peers)

    def direct(s):
        return pltpu.make_async_remote_copy(
            src_ref=ham, dst_ref=w[mid - 2 * s], send_sem=send.at[s + R], recv_sem=recv.at[mid - 2 * s],
            device_id=(me + 2 * s,), device_id_type=MESH)

    def arrived(r):
        pltpu.make_async_remote_copy(
            src_ref=ham, dst_ref=w[r], send_sem=send.at[0], recv_sem=recv.at[r],
            device_id=(sib,), device_id_type=MESH).wait_recv()

    def passed(s, d):
        r = mid + 2 * s - d
        return pltpu.make_async_remote_copy(
            src_ref=ham if s == 0 else w[mid + 2 * s], dst_ref=w[r], send_sem=fsend.at[s + R],
            recv_sem=recv.at[r], device_id=(sib,), device_id_type=MESH)

    def pass_on(s, act):
        for d in (1, -1):
            if 0 <= mid + 2 * s - d < WIDE:
                @pl.when((delta == d) & inside(me + 2 * s))
                def _(d=d):
                    act(passed(s, d))

    pass_on(0, lambda c: c.start())
    for s in steps:
        @pl.when(inside(me + 2 * s))
        def _(s=s):
            direct(s).start()

    zero = jnp.zeros((b, b), jnp.bfloat16)
    for q in range(COLS):
        band[q, 0:b, :] = zero
        band[q, (TALL - 1) * b:, :] = zero

    def spread(r):
        src = ham if r == mid else w[r]
        for d in range(SPAN):
            slot = inv[r * SPAN + d]
            block = src[jnp.maximum(slot, 0)]
            band[r + d, (SPAN - d) * b:(SPAN + 1 - d) * b, :] = jnp.where(slot >= 0, block, zero)

    def fetch(r):
        if r % 2 == 0:
            s = (r - mid) // 2
            @pl.when(inside(me + 2 * s))
            def _():
                arrived(r)
            pass_on(s, lambda c: c.start())
        else:
            @pl.when(inside(me + r - mid))
            def _():
                arrived(r)

    ident = jnp.where(
        lax.broadcasted_iota(jnp.int32, (b, b), 0) == lax.broadcasted_iota(jnp.int32, (b, b), 1), 1.0, 0.0)

    def second(t):
        left = jnp.concatenate(
            [band[t + R + d, (SPAN - d) * b:(SPAN + 1 - d) * b, :] for d in range(SPAN)], axis=1)
        for e in range(0, WIDE, 2):
            es = [e] if e + 1 == WIDE else [e, e + 1]
            lo, hi = max(0, e - SPAN + 1), min(SPAN - 1, es[-1])
            right = jnp.concatenate(
                [band[t + x, (lo - x + SPAN) * b:(hi - x + SPAN + 1) * b, :] for x in es], axis=1)
            prod = jnp.dot(left[:, lo * b:(hi + 1) * b], right, preferred_element_type=jnp.float32)
            for n, x in enumerate(es):
                got = 2.0 * prod[:, n * b:(n + 1) * b]
                if x == 2 * R:
                    got = got - ident
                t2[t * WIDE + x] = got.astype(jnp.bfloat16)

    spread(mid)
    for r in sorted((x for x in range(R, 3 * R + 1) if x != mid and x % 2 == 0), key=lambda x: abs(x - mid)):
        fetch(r)
        spread(r)
    for r in sorted((x for x in range(R, 3 * R + 1) if x % 2), key=lambda x: abs(x - mid)):
        fetch(r)
        spread(r)
    second(R)
    for u in range(1, R + 1):
        if u % 2:
            for r in (R - u - 1, 3 * R + u + 1, R - u, 3 * R + u):
                fetch(r)
        for r in (R - u, 3 * R + u):
            spread(r)

        @pl.loop(0, 2)
        def _(j, u=u):
            second(R - u + 2 * u * j)

    left = jnp.concatenate(
        [band[2 * R + d, (SPAN - d) * b:(SPAN + 1 - d) * b, :] for d in range(SPAN)], axis=1)
    c0, c1, c2, c3 = coefs[0], coefs[1], coefs[2], coefs[3]

    def column(g, t):
        e = tidx[g * SPAN + t]
        return jnp.where(e >= 0, t2[t * WIDE + jnp.maximum(e, 0)], zero)

    @pl.loop(0, kb // 2)
    def _(p):
        gs = [2 * p, 2 * p + 1]
        right = jnp.concatenate(
            [jnp.concatenate([column(g, t) for t in range(SPAN)], axis=0) for g in gs], axis=1)
        prod = jnp.dot(left, right, preferred_element_type=jnp.float32)
        for n, g in enumerate(gs):
            slot = slot1[g]
            one = jnp.where(slot >= 0, ham[jnp.maximum(slot, 0)], zero).astype(jnp.float32)
            two = column(g, R).astype(jnp.float32)
            start = jnp.where(diag[g] > 0, ident, 0.0)
            out[g] = c0 * start + c1 * one + c2 * two + c3 * (2.0 * prod[:, n * b:(n + 1) * b] - one)

    for s in steps:
        @pl.when(inside(me + 2 * s))
        def _(s=s):
            direct(s).wait_send()
    for s in [0] + steps:
        pass_on(s, lambda c: c.wait_send())


def body(ham, hpat, kpat, coefs):
    own = lax.axis_index("rows")
    count = lax.axis_size("rows")
    _, hb, b, _ = ham.shape
    kb = kpat.shape[1]
    hrows = lax.dynamic_slice(
        jnp.pad(hpat, ((2 * R, 2 * R), (0, 0)), constant_values=-1), (own, 0), (WIDE, hb))
    cols = own - 3 * R + jnp.arange(WIDE)[:, None] + jnp.arange(SPAN)[None, :]
    hit = (hrows[:, None, :] == cols[:, :, None]) & (cols >= 0)[:, :, None]
    inv = jnp.max(jnp.where(hit, jnp.arange(hb), -1), axis=2).reshape(-1)
    krows = lax.dynamic_slice(
        jnp.pad(kpat, ((R, R), (0, 0)), constant_values=-1), (own, 0), (SPAN, kb))
    row_k, row_h = krows[R], hrows[2 * R]
    far = row_k[:, None] - (own - R + jnp.arange(SPAN))[None, :] + 2 * R
    held = jnp.any(krows[None, :, :] == row_k[:, None, None], axis=2)
    tidx = jnp.where(held & (row_k >= 0)[:, None] & (far >= 0) & (far < WIDE), far, -1).reshape(-1)
    one = (row_h[None, :] == row_k[:, None]) & (row_k >= 0)[:, None]
    slot1 = jnp.max(jnp.where(one, jnp.arange(hb), -1), axis=1)
    diag = (row_k == own).astype(jnp.int32)
    smem = pl.BlockSpec(memory_space=pltpu.SMEM)
    vmem = pl.BlockSpec(memory_space=pltpu.VMEM)
    row = pltpu.VMEM((hb, b, b), jnp.bfloat16)
    got = pl.pallas_call(
        functools.partial(kernel, count),
        out_shape=jax.ShapeDtypeStruct((kb, b, b), jnp.float32),
        in_specs=[smem] * 5 + [vmem],
        out_specs=vmem,
        scratch_shapes=[row] * WIDE + [
            pltpu.VMEM((COLS, TALL * b, b), jnp.bfloat16),
            pltpu.VMEM((SPAN * WIDE, b, b), jnp.bfloat16),
            pltpu.SemaphoreType.DMA((SPAN,)),
            pltpu.SemaphoreType.DMA((SPAN,)),
            pltpu.SemaphoreType.DMA((WIDE,)),
        ],
        compiler_params=pltpu.CompilerParams(
            collective_id=0, has_side_effects=True, vmem_limit_bytes=56 * 1024 * 1024),
        cost_estimate=pl.CostEstimate(flops=10**10, bytes_accessed=10**7, transcendentals=0),
    )(coefs, inv, tidx, slot1, diag, ham[0])
    return got[None]


def solution(mesh):
    in_specs = (P("rows", None, None, None), P(), P(), P())
    out_specs = P("rows", None, None, None)
    return jax.shard_map(body, mesh=mesh, in_specs=in_specs, out_specs=out_specs, check_vma=False)
```

time: 508 us -> 103 us (0.20)
  the two profiles are of different devices: /device:TPU:18 before, /device:TPU:7 now
where the time goes in v1:
time: 103 us
  Pallas kernels  92.9 us (90%)
  local copies, waits for them, and re-layouts  6.53 us (6%)
  other arithmetic  3.05 us (3%)
    pallas_call x1, Pallas kernels, body(): pl.pallas_call(functools.partial(kernel, count), out_shape=jax.ShapeDtype...  92.9 us
    unnamed x1, local copies, waits for them, and re-layouts  3.02 us

profile of v1, /device:TPU:7, one launch (start us, length us, event | category | flops | bytes accessed | tf_op | source)
XLA Modules:
  0.0 102.5 jit_solution(10059995870695842416)
XLA Ops:
  0.0 0.9 dynamic-slice_reduce_fusion
  0.9 1.3 %compare_convert_fusion = (s32[30]{0:T(128)}, s32[30]{0:T(128)S(1)}) fusion(s32[]{:T(128)S(6)} %axis_index.12, s32[]{:T(128)S(6)} %add.76, s32[32,30]{1,0:T(8,128)} %param.6), kind=kLoop, calls=%fused_computation.11 | loop fusion | flops 60 | bytes 4088 | tf_op jit(solution)/shard_map/convert_element_type | solution.py:178
  2.2 0.6 select_reduce_fusion.1.slot1
  2.8 0.8 pad_dynamic-slice_fusion.2
  3.7 0.7 pad_dynamic-slice_fusion.1
  4.4 0.4 compare_reduce_fusion
  4.8 0.1 copy.8
  4.9 0.1 and.41
  5.0 0.1 copy.7
  5.1 0.7 reshape.69.inv
  5.8 0.1 subtract_add_fusion
  5.9 0.1 add.74
  6.0 0.6 and_select_fusion.tidx
  6.6 92.9 %shard_map.46 = f32[30,128,128]{2,1,0:T(8,128)} custom-call(f32[4]{0:T(128)} %coefs.1, s32[325]{0:T(512)} %reshape.69.inv, s32[390]{0:T(512)} %and_select_fusion.tidx, s32[30]{0:T(128)} %select_reduce_fusion.1.slot1, s32[30]{0:T(128)} %get-tuple-element.5.diag, bf16[10,128,128]{2,1,0:T(8,128)(2,1)} %bitcast.6), custom_call_target="tpu_custom_call" | custom-call | flops 10000000000 | bytes 10000000 | tf_op jit(solution)/shard_map/pallas_call | solution.py:182
  99.5 3.0 %copy.10 = f32[1,30,128,128]{3,2,1,0:T(8,128)} copy(f32[1,30,128,128]{3,2,1,0:T(8,128)} %bitcast.5) | data formatting | bytes 3932160
  (7 shorter events, 0.1 us)

commit v2 on v1

--- a/solution.py
+++ b/solution.py
@@ -28,44 +28,107 @@
     def inside(row):
         return (row >= 0) & (row < count)
 
+    chip = lax.div(me, 2)
+    place = lax.rem(chip, 4)
+    hb = ham.shape[0]
+    cut = hb // 2
+    halves = [(0, cut), (cut, hb - cut)]
+
+    def inside(row):
+        return (row >= 0) & (row < count)
+
     barrier = pltpu.get_barrier_semaphore()
+    near = [me + 2 * (1 - 2 * lax.rem(place, 2)), me + 4 * (1 - 2 * lax.div(place, 2)), me + 8, me - 8]
     pl.semaphore_signal(barrier, inc=1, device_id=(sib,), device_id_type=MESH)
-    steps = [s * sign for s in range(1, R + 1) for sign in (1, -1)]
-    for s in steps:
-        @pl.when(inside(me + 2 * s))
-        def _(s=s):
-            pl.semaphore_signal(barrier, inc=1, device_id=(me + 2 * s,), device_id_type=MESH)
-    peers = 1 + sum(jnp.where(inside(me + 2 * s), 1, 0) for s in steps)
+    for other in near:
+        @pl.when(inside(other))
+        def _(other=other):
+            pl.semaphore_signal(barrier, inc=1, device_id=(other,), device_id_type=MESH)
+    peers = 1 + sum(jnp.where(inside(other), 1, 0) for other in near)
     pl.semaphore_wait(barrier, peers)
 
-    def direct(s):
+    def part(ref, n):
+        return ref.at[pl.ds(*halves[n])]
+
+    def row_ref(s):
+        return ham if s == 0 else w[mid + 2 * s]
+
+    def relay(s, n, link, step):
+        r = mid + 2 * (s - step)
         return pltpu.make_async_remote_copy(
-            src_ref=ham, dst_ref=w[mid - 2 * s], send_sem=send.at[s + R], recv_sem=recv.at[mid - 2 * s],
-            device_id=(me + 2 * s,), device_id_type=MESH)
-
-    def arrived(r):
+            src_ref=part(row_ref(s), n), dst_ref=part(w[r], n), send_sem=send.at[(s + R) * 8 + link * 2 + n],
+            recv_sem=recv.at[2 * r + n], device_id=(me + 2 * step,), device_id_type=MESH)
+
+    def arrived(r, n):
         pltpu.make_async_remote_copy(
-            src_ref=ham, dst_ref=w[r], send_sem=send.at[0], recv_sem=recv.at[r],
+            src_ref=part(ham, n), dst_ref=part(w[r], n), send_sem=fsend.at[0], recv_sem=recv.at[2 * r + n],
             device_id=(sib,), device_id_type=MESH).wait_recv()
 
-    def passed(s, d):
-        r = mid + 2 * s - d
-        return pltpu.make_async_remote_copy(
-            src_ref=ham if s == 0 else w[mid + 2 * s], dst_ref=w[r], send_sem=fsend.at[s + R],
-            recv_sem=recv.at[r], device_id=(sib,), device_id_type=MESH)
-
-    def pass_on(s, act):
+    def pass_on(s, n, act):
         for d in (1, -1):
-            if 0 <= mid + 2 * s - d < WIDE:
-                @pl.when((delta == d) & inside(me + 2 * s))
-                def _(d=d):
-                    act(passed(s, d))
-
-    pass_on(0, lambda c: c.start())
-    for s in steps:
-        @pl.when(inside(me + 2 * s))
-        def _(s=s):
-            direct(s).start()
+            r = mid + 2 * s - d
+            if 0 <= r < WIDE:
+                @pl.when(delta == d)
+                def _(r=r):
+                    act(pltpu.make_async_remote_copy(
+                        src_ref=part(row_ref(s), n), dst_ref=part(w[r], n), send_sem=fsend.at[2 * (s + R) + n],
+                        recv_sem=recv.at[2 * r + n], device_id=(sib,), device_id_type=MESH))
+
+    def route(o, s, n):
+        if s == 0:
+            return 0, 0
+        z, p = (o + s) // 4, (o + s) % 4
+        x, y = (o ^ 1) - o, (o ^ 2) - o
+        if z == 0:
+            if p == o ^ 3:
+                return (x if n == 0 else y), 2
+            return s, 1
+        sign = 1 if z > 0 else -1
+        if abs(z) == 1 and p in (o ^ 1, o ^ 2):
+            step = x if p == o ^ 1 else y
+            return step, 2
+        step = 4 * sign
+        if s == step:
+            return step, 1
+        return step, route(o, s - step, n)[1] + 1
+
+    def sends(o, s, n):
+        out_steps = []
+        for link, step in enumerate(((o ^ 1) - o, (o ^ 2) - o, 4, -4)):
+            t = s - step
+            if t != 0 and abs(t) <= R and route((o + step) % 4, t, n)[0] == -step:
+                out_steps.append((link, step))
+        return out_steps
+
+    def plan(o):
+        keys = [(route(o, s, n)[1], n, abs(s), s) for s in range(-R, R + 1) for n in (0, 1)]
+        return [(h, s, n) for h, n, _, s in sorted(keys)]
+
+    def ship(o, s, n, act):
+        for link, step in sends(o, s, n):
+            @pl.when(inside(me + 2 * step))
+            def _(link=link, step=step):
+                act(relay(s, n, link, step))
+        pass_on(s, n, act)
+
+    def each_place(f):
+        for o in range(4):
+            @pl.when(place == o)
+            def _(o=o):
+                f(o)
+
+    def level(hops):
+        def go(o):
+            for h, s, n in plan(o):
+                if h in hops:
+                    @pl.when(inside(me + 2 * s))
+                    def _(s=s, n=n):
+                        if h > 0:
+                            arrived(mid + 2 * s, n)
+                        ship(o, s, n, lambda c: c.start())
+        each_place(go)
+
+    level((0,))
 
     zero = jnp.zeros((b, b), jnp.bfloat16)
     for q in range(COLS):
@@ -80,16 +143,10 @@
             band[r + d, (SPAN - d) * b:(SPAN + 1 - d) * b, :] = jnp.where(slot >= 0, block, zero)
 
     def fetch(r):
-        if r % 2 == 0:
-            s = (r - mid) // 2
-            @pl.when(inside(me + 2 * s))
-            def _():
-                arrived(r)
-            pass_on(s, lambda c: c.start())
-        else:
-            @pl.when(inside(me + r - mid))
-            def _():
-                arrived(r)
+        @pl.when(inside(me + r - mid))
+        def _():
+            for n in (0, 1):
+                arrived(r, n)
 
     ident = jnp.where(
         lax.broadcasted_iota(jnp.int32, (b, b), 0) == lax.broadcasted_iota(jnp.int32, (b, b), 1), 1.0, 0.0)
@@ -110,23 +167,18 @@
                 t2[t * WIDE + x] = got.astype(jnp.bfloat16)
 
     spread(mid)
-    for r in sorted((x for x in range(R, 3 * R + 1) if x != mid and x % 2 == 0), key=lambda x: abs(x - mid)):
-        fetch(r)
-        spread(r)
-    for r in sorted((x for x in range(R, 3 * R + 1) if x % 2), key=lambda x: abs(x - mid)):
-        fetch(r)
-        spread(r)
-    second(R)
-    for u in range(1, R + 1):
-        if u % 2:
-            for r in (R - u - 1, 3 * R + u + 1, R - u, 3 * R + u):
-                fetch(r)
-        for r in (R - u, 3 * R + u):
+    level((1,))
+    level((2,))
+    level((3, 4))
+    for r in range(WIDE):
+        if r % 2:
+            fetch(r)
+        if r != mid:
             spread(r)
 
-        @pl.loop(0, 2)
-        def _(j, u=u):
-            second(R - u + 2 * u * j)
+    @pl.loop(0, SPAN)
+    def _(t):
+        second(t)
 
     left = jnp.concatenate(
         [band[2 * R + d, (SPAN - d) * b:(SPAN + 1 - d) * b, :] for d in range(SPAN)], axis=1)
@@ -149,12 +201,13 @@
             start = jnp.where(diag[g] > 0, ident, 0.0)
             out[g] = c0 * start + c1 * one + c2 * two + c3 * (2.0 * prod[:, n * b:(n + 1) * b] - one)
 
-    for s in steps:
-        @pl.when(inside(me + 2 * s))
-        def _(s=s):
-            direct(s).wait_send()
-    for s in [0] + steps:
-        pass_on(s, lambda c: c.wait_send())
+    def drain(o):
+        for _, s, n in plan(o):
+            @pl.when(inside(me + 2 * s))
+            def _(s=s, n=n):
+                ship(o, s, n, lambda c: c.wait_send())
+
+    each_place(drain)
 
 
 def body(ham, hpat, kpat, coefs):
@@ -187,9 +240,9 @@
         scratch_shapes=[row] * WIDE + [
             pltpu.VMEM((COLS, TALL * b, b), jnp.bfloat16),
             pltpu.VMEM((SPAN * WIDE, b, b), jnp.bfloat16),
-            pltpu.SemaphoreType.DMA((SPAN,)),
-            pltpu.SemaphoreType.DMA((SPAN,)),
-            pltpu.SemaphoreType.DMA((WIDE,)),
+            pltpu.SemaphoreType.DMA((SPAN * 8,)),
+            pltpu.SemaphoreType.DMA((SPAN * 2,)),
+            pltpu.SemaphoreType.DMA((WIDE * 2,)),
         ],
         compiler_params=pltpu.CompilerParams(
             collective_id=0, has_side_effects=True, vmem_limit_bytes=56 * 1024 * 1024),

time: 103 us -> 77.8 us (0.76)
  Pallas kernels: 92.9 us -> 67.1 us
    pallas_call x1, Pallas kernels: 92.9 us -> 67.1 us  [body(): pl.pallas_call(functools.partial(kernel, count), out_shape=jax.ShapeDtype...]
where the time goes in v2:
time: 77.8 us; the launch traced here: 76.8 us
  Pallas kernels  67.1 us (86%)
  local copies, waits for them, and re-layouts  6.53 us (8%)
  other arithmetic  3.05 us (4%)
    pallas_call x1, Pallas kernels, body(): pl.pallas_call(functools.partial(kernel, count), out_shape=jax.ShapeDtype...  67.1 us
    unnamed x1, local copies, waits for them, and re-layouts  3.02 us

profile of v2, /device:TPU:7, one launch (start us, length us, event | category | flops | bytes accessed | tf_op | source)
XLA Modules:
  0.0 76.8 jit_solution(4898791828745850769)
XLA Ops:
  0.0 0.9 %dynamic-slice_reduce_fusion = s32[10]{0:T(128)S(1)} fusion(s32[]{:T(128)S(6)} %add.77, s32[32,10]{0,1:T(8,128)} %param.5), kind=kLoop, calls=%fused_computation.5 | loop fusion | bytes 1324 | tf_op jit(solution)/shard_map/slice | solution.py:225
  0.9 1.3 %compare_convert_fusion = (s32[30]{0:T(128)}, s32[30]{0:T(128)S(1)}) fusion(s32[]{:T(128)S(6)} %axis_index.12, s32[]{:T(128)S(6)} %add.76, s32[32,30]{1,0:T(8,128)} %param.6), kind=kLoop, calls=%fused_computation.11 | loop fusion | flops 60 | bytes 4088 | tf_op jit(solution)/shard_map/convert_element_type | solution.py:231
  2.2 0.6 select_reduce_fusion.1.slot1
  2.8 0.8 %pad_dynamic-slice_fusion.2 = s32[25,10]{0,1:T(8,128)S(1)} fusion(s32[]{:T(128)S(6)} %select_n.19, s32[32,10]{0,1:T(8,128)} %param.5), kind=kLoop, calls=%fused_computation.8 | loop fusion | bytes 2284 | tf_op jit(solution)/shard_map/dynamic_slice | solution.py:218
  3.7 0.7 pad_dynamic-slice_fusion.1
  4.4 0.4 compare_reduce_fusion
  4.8 0.1 copy.8
  4.9 0.1 and.41
  5.0 0.1 copy.7
  5.1 0.7 reshape.69.inv
  5.8 0.1 subtract_add_fusion
  5.9 0.1 add.74
  6.0 0.6 and_select_fusion.tidx
  6.6 67.1 %shard_map.46 = f32[30,128,128]{2,1,0:T(8,128)} custom-call(f32[4]{0:T(128)} %coefs.1, s32[325]{0:T(512)} %reshape.69.inv, s32[390]{0:T(512)} %and_select_fusion.tidx, s32[30]{0:T(128)} %select_reduce_fusion.1.slot1, s32[30]{0:T(128)} %get-tuple-element.5.diag, bf16[10,128,128]{2,1,0:T(8,128)(2,1)} %bitcast.6), custom_call_target="tpu_custom_call" | custom-call | flops 10000000000 | bytes 10000000 | tf_op jit(solution)/shard_map/pallas_call | solution.py:235
  73.7 3.0 %copy.10 = f32[1,30,128,128]{3,2,1,0:T(8,128)} copy(f32[1,30,128,128]{3,2,1,0:T(8,128)} %bitcast.5) | data formatting | bytes 3932160
  (7 shorter events, 0.1 us)

commit v3 on v2

--- a/solution.py
+++ b/solution.py
@@ -15,9 +15,9 @@
 MESH = pl.DeviceIdType.MESH
 
 
-def kernel(count, coefs, inv, tidx, slot1, diag, ham, out, *scratch):
+def kernel(count, coefs, hpat, kpat, ham, out, *scratch):
     w = scratch[:WIDE]
-    band, t2, send, fsend, recv = scratch[WIDE:]
+    band, t2, slots, used, send, fsend, recv = scratch[WIDE:]
     b = ham.shape[-1]
     kb = out.shape[0]
     mid = 2 * R
@@ -84,9 +84,15 @@
                 return (x if n == 0 else y), 2
             return s, 1
         sign = 1 if z > 0 else -1
+        flat = 1 if o in (0, 1) else -1
+        if o in (0, 3) and p == o ^ 3 and z == -flat and n == 1:
+            return y, route(o ^ 2, s - y, n)[1] + 1
+        if o in (0, 3) and p == o ^ 3 and z == -2 * flat and n == 0:
+            return x, route(o ^ 1, s - x, n)[1] + 1
         if abs(z) == 1 and p in (o ^ 1, o ^ 2):
-            step = x if p == o ^ 1 else y
-            return step, 2
+            if z == flat and (o in (0, 3) or n == (0 if p == o ^ 1 else 1)):
+                return 4 * sign, route(o, s - 4 * sign, n)[1] + 1
+            return (x if p == o ^ 1 else y), 2
         step = 4 * sign
         if s == step:
             return step, 1
@@ -135,10 +141,35 @@
         band[q, 0:b, :] = zero
         band[q, (TALL - 1) * b:, :] = zero
 
+    def find(named, col):
+        slot = jnp.int32(-1)
+        for h in range(hb):
+            slot = jnp.where(named[h] == col, h, slot)
+        return slot
+
+    @pl.loop(0, WIDE)
+    def _(r):
+        row = me + r - mid
+        named = [hpat[jnp.clip(row, 0, count - 1), h] for h in range(hb)]
+        for d in range(SPAN):
+            col = row - R + d
+            slots[r * SPAN + d] = jnp.where(inside(row) & (col >= 0), find(named, col), -1)
+
+    @pl.loop(0, SPAN)
+    def _(t):
+        row = me - R + t
+        word = jnp.int32(0)
+        for u in range(kb):
+            col = kpat[jnp.clip(row, 0, count - 1), u]
+            e = col - row + 2 * R
+            ok = (col >= 0) & (e >= 0) & (e < WIDE) & inside(row)
+            word = word | jnp.where(ok, jnp.left_shift(1, jnp.clip(e, 0, WIDE - 1)), 0)
+        used[t] = word
+
     def spread(r):
         src = ham if r == mid else w[r]
         for d in range(SPAN):
-            slot = inv[r * SPAN + d]
+            slot = slots[r * SPAN + d]
             block = src[jnp.maximum(slot, 0)]
             band[r + d, (SPAN - d) * b:(SPAN + 1 - d) * b, :] = jnp.where(slot >= 0, block, zero)
 
@@ -151,7 +182,8 @@
     ident = jnp.where(
         lax.broadcasted_iota(jnp.int32, (b, b), 0) == lax.broadcasted_iota(jnp.int32, (b, b), 1), 1.0, 0.0)
 
-    def second(t):
+    def second(h):
+        t = jnp.clip(hpat[me, h] - me + R, 0, SPAN - 1)
         left = jnp.concatenate(
             [band[t + R + d, (SPAN - d) * b:(SPAN + 1 - d) * b, :] for d in range(SPAN)], axis=1)
         for e in range(0, WIDE, 2):
@@ -164,41 +196,68 @@
                 got = 2.0 * prod[:, n * b:(n + 1) * b]
                 if x == 2 * R:
                     got = got - ident
-                t2[t * WIDE + x] = got.astype(jnp.bfloat16)
+                t2[h * WIDE + x] = got.astype(jnp.bfloat16)
 
     spread(mid)
     level((1,))
     level((2,))
-    level((3, 4))
-    for r in range(WIDE):
+
+    def soon(r):
+        got = False
+        for o in range(4):
+            for d in (1, -1):
+                if r % 2 or d == 1:
+                    s = (r - mid - (d if r % 2 else 0)) // 2
+                    if abs(s) <= R and max(route(o, s, 0)[1], route(o, s, 1)[1]) <= 2:
+                        here = place == o
+                        got = got | ((here & (delta == d)) if r % 2 else here)
+        return got
+
+    def settle(r):
         if r % 2:
             fetch(r)
-        if r != mid:
-            spread(r)
-
-    @pl.loop(0, SPAN)
-    def _(t):
-        second(t)
-
-    left = jnp.concatenate(
-        [band[2 * R + d, (SPAN - d) * b:(SPAN + 1 - d) * b, :] for d in range(SPAN)], axis=1)
+        spread(r)
+
+    others = [r for r in range(WIDE) if r != mid]
+    for r in others:
+        @pl.when(soon(r))
+        def _(r=r):
+            settle(r)
+    level((3, 4, 5))
+    for r in others:
+        @pl.when(jnp.logical_not(soon(r)))
+        def _(r=r):
+            settle(r)
+
+    @pl.loop(0, hb)
+    def _(h):
+        second(h)
+
+    left = jnp.concatenate([ham[h] for h in range(hb)], axis=1)
     c0, c1, c2, c3 = coefs[0], coefs[1], coefs[2], coefs[3]
 
-    def column(g, t):
-        e = tidx[g * SPAN + t]
-        return jnp.where(e >= 0, t2[t * WIDE + jnp.maximum(e, 0)], zero)
+    named = [hpat[me, h] for h in range(hb)]
+    words = [used[jnp.clip(named[h] - me + R, 0, SPAN - 1)] for h in range(hb)]
+
+    def column(col, h):
+        e = col - named[h] + 2 * R
+        at = jnp.clip(e, 0, WIDE - 1)
+        ok = (named[h] >= 0) & (col >= 0) & (e == at) & ((jnp.right_shift(words[h], at) & 1) == 1)
+        return jnp.where(ok, t2[h * WIDE + at], zero)
 
     @pl.loop(0, kb // 2)
     def _(p):
         gs = [2 * p, 2 * p + 1]
+        cols = [kpat[me, g] for g in gs]
         right = jnp.concatenate(
-            [jnp.concatenate([column(g, t) for t in range(SPAN)], axis=0) for g in gs], axis=1)
+            [jnp.concatenate([column(col, h) for h in range(hb)], axis=0) for col in cols], axis=1)
         prod = jnp.dot(left, right, preferred_element_type=jnp.float32)
         for n, g in enumerate(gs):
-            slot = slot1[g]
+            col = cols[n]
+            slot = jnp.where(col >= 0, find(named, col), -1)
             one = jnp.where(slot >= 0, ham[jnp.maximum(slot, 0)], zero).astype(jnp.float32)
-            two = column(g, R).astype(jnp.float32)
-            start = jnp.where(diag[g] > 0, ident, 0.0)
+            two = column(col, 0).astype(jnp.float32)
+            start = jnp.where(col == me, ident, 0.0)
             out[g] = c0 * start + c1 * one + c2 * two + c3 * (2.0 * prod[:, n * b:(n + 1) * b] - one)
 
     def drain(o):
@@ -211,35 +270,22 @@
 
 
 def body(ham, hpat, kpat, coefs):
-    own = lax.axis_index("rows")
     count = lax.axis_size("rows")
     _, hb, b, _ = ham.shape
     kb = kpat.shape[1]
-    hrows = lax.dynamic_slice(
-        jnp.pad(hpat, ((2 * R, 2 * R), (0, 0)), constant_values=-1), (own, 0), (WIDE, hb))
-    cols = own - 3 * R + jnp.arange(WIDE)[:, None] + jnp.arange(SPAN)[None, :]
-    hit = (hrows[:, None, :] == cols[:, :, None]) & (cols >= 0)[:, :, None]
-    inv = jnp.max(jnp.where(hit, jnp.arange(hb), -1), axis=2).reshape(-1)
-    krows = lax.dynamic_slice(
-        jnp.pad(kpat, ((R, R), (0, 0)), constant_values=-1), (own, 0), (SPAN, kb))
-    row_k, row_h = krows[R], hrows[2 * R]
-    far = row_k[:, None] - (own - R + jnp.arange(SPAN))[None, :] + 2 * R
-    held = jnp.any(krows[None, :, :] == row_k[:, None, None], axis=2)
-    tidx = jnp.where(held & (row_k >= 0)[:, None] & (far >= 0) & (far < WIDE), far, -1).reshape(-1)
-    one = (row_h[None, :] == row_k[:, None]) & (row_k >= 0)[:, None]
-    slot1 = jnp.max(jnp.where(one, jnp.arange(hb), -1), axis=1)
-    diag = (row_k == own).astype(jnp.int32)
     smem = pl.BlockSpec(memory_space=pltpu.SMEM)
     vmem = pl.BlockSpec(memory_space=pltpu.VMEM)
     row = pltpu.VMEM((hb, b, b), jnp.bfloat16)
     got = pl.pallas_call(
         functools.partial(kernel, count),
         out_shape=jax.ShapeDtypeStruct((kb, b, b), jnp.float32),
-        in_specs=[smem] * 5 + [vmem],
+        in_specs=[smem] * 3 + [vmem],
         out_specs=vmem,
         scratch_shapes=[row] * WIDE + [
             pltpu.VMEM((COLS, TALL * b, b), jnp.bfloat16),
-            pltpu.VMEM((SPAN * WIDE, b, b), jnp.bfloat16),
+            pltpu.VMEM((hb * WIDE, b, b), jnp.bfloat16),
+            pltpu.SMEM((WIDE * SPAN,), jnp.int32),
+            pltpu.SMEM((SPAN,), jnp.int32),
             pltpu.SemaphoreType.DMA((SPAN * 8,)),
             pltpu.SemaphoreType.DMA((SPAN * 2,)),
             pltpu.SemaphoreType.DMA((WIDE * 2,)),
@@ -247,7 +293,7 @@
         compiler_params=pltpu.CompilerParams(
             collective_id=0, has_side_effects=True, vmem_limit_bytes=56 * 1024 * 1024),
         cost_estimate=pl.CostEstimate(flops=10**10, bytes_accessed=10**7, transcendentals=0),
-    )(coefs, inv, tidx, slot1, diag, ham[0])
+    )(coefs, hpat, kpat, ham[0])
     return got[None]
 
 

time: 77.8 us -> 59.5 us (0.76); the launches traced: 76.8 us -> 59.3 us
  Pallas kernels: 67.1 us -> 54.9 us
  other arithmetic: 3.05 us -> 0 us
  local copies, waits for them, and re-layouts: 6.53 us -> 4.4 us
    pallas_call x1, Pallas kernels: 67.1 us -> 54.9 us  [body(): pl.pallas_call(functools.partial(kernel, count), out_shape=jax.ShapeDtype...]
    dynamic_slice x2 -> x0, local copies, waits for them, and re-layouts: 1.52 us -> none  [the longest x1 0.78 us: body(): lax.dynamic_slice(jnp.pad(hpat, ((2 * R, 2 * R), (0, 0)), constant_values...]
    unnamed x1 -> x2, local copies, waits for them, and re-layouts: 3.02 us -> 4.4 us
    convert_element_type x1 -> x0, other arithmetic: 1.29 us -> none  [body(): diag = (row_k == own).astype(jnp.int32)]
    slice x1 -> x0, local copies, waits for them, and re-layouts: 0.88 us -> none  [body(): row_k, row_h = (krows[R], hrows[2 * R])]
where the time goes in v3:
time: 59.5 us; the launch traced here: 59.3 us
  Pallas kernels  54.9 us (92%)
  local copies, waits for them, and re-layouts  4.4 us (7%)
    pallas_call x1, Pallas kernels, body(): pl.pallas_call(functools.partial(kernel, count), out_shape=jax.ShapeDtype...  54.9 us
    unnamed x2, local copies, waits for them, and re-layouts  4.4 us

profile of v3, /device:TPU:7, one launch (start us, length us, event | category | flops | bytes accessed | tf_op | source)
XLA Modules:
  0.0 59.3 jit_solution(4666929919215486935)
XLA Ops:
  0.0 1.4 %copy.5.hpat = s32[32,10]{1,0:T(8,128)} copy(s32[32,10]{0,1:T(8,128)} %param.5) | data formatting | bytes 2560 | tf_op args[1]
  1.4 54.9 %shard_map.46 = f32[30,128,128]{2,1,0:T(8,128)} custom-call(f32[4]{0:T(128)} %coefs.1, s32[32,10]{1,0:T(8,128)} %copy.5.hpat, s32[32,30]{1,0:T(8,128)} %kpat.1, bf16[10,128,128]{2,1,0:T(8,128)(2,1)} %bitcast.3), custom_call_target="tpu_custom_call" | custom-call | flops 10000000000 | bytes 10000000 | tf_op jit(solution)/shard_map/pallas_call | solution.py:279
  56.3 3.0 %copy.7 = f32[1,30,128,128]{3,2,1,0:T(8,128)} copy(f32[1,30,128,128]{3,2,1,0:T(8,128)} %bitcast.2) | data formatting | bytes 3932160

commit v4 on v3

--- a/solution.py
+++ b/solution.py
@@ -245,8 +245,7 @@
         ok = (named[h] >= 0) & (col >= 0) & (e == at) & ((jnp.right_shift(words[h], at) & 1) == 1)
         return jnp.where(ok, t2[h * WIDE + at], zero)
 
-    @pl.loop(0, kb // 2)
-    def _(p):
+    def third(p):
         gs = [2 * p, 2 * p + 1]
         cols = [kpat[me, g] for g in gs]
         right = jnp.concatenate(
@@ -259,6 +258,14 @@
             two = column(col, 0).astype(jnp.float32)
             start = jnp.where(col == me, ident, 0.0)
             out[g] = c0 * start + c1 * one + c2 * two + c3 * (2.0 * prod[:, n * b:(n + 1) * b] - one)
+
+    pairs = kb // 2
+    group = 3 if pairs % 3 == 0 else 1
+
+    @pl.loop(0, pairs // group)
+    def _(p):
+        for n in range(group):
+            third(p * group + n)
 
     def drain(o):
         for _, s, n in plan(o):

time: 59.5 us -> 58.1 us (0.976)
  Pallas kernels: 54.9 us -> 53.4 us
    pallas_call x1, Pallas kernels: 54.9 us -> 53.4 us  [body(): pl.pallas_call(functools.partial(kernel, count), out_shape=jax.ShapeDtype...]
where the time goes in v4:
time: 58.1 us; the launch traced here: 57.9 us
  Pallas kernels  53.4 us (92%)
  local copies, waits for them, and re-layouts  4.4 us (8%)
    pallas_call x1, Pallas kernels, body(): pl.pallas_call(functools.partial(kernel, count), out_shape=jax.ShapeDtype...  53.4 us
    unnamed x2, local copies, waits for them, and re-layouts  4.4 us

profile of v4, /device:TPU:7, one launch (start us, length us, event | category | flops | bytes accessed | tf_op | source)
XLA Modules:
  0.0 57.9 jit_solution(10723054774028538254)
XLA Ops:
  0.0 1.4 %copy.5.hpat = s32[32,10]{1,0:T(8,128)} copy(s32[32,10]{0,1:T(8,128)} %param.5) | data formatting | bytes 2560 | tf_op args[1]
  1.4 53.4 %shard_map.46 = f32[30,128,128]{2,1,0:T(8,128)} custom-call(f32[4]{0:T(128)} %coefs.1, s32[32,10]{1,0:T(8,128)} %copy.5.hpat, s32[32,30]{1,0:T(8,128)} %kpat.1, bf16[10,128,128]{2,1,0:T(8,128)(2,1)} %bitcast.3), custom_call_target="tpu_custom_call" | custom-call | flops 10000000000 | bytes 10000000 | tf_op jit(solution)/shard_map/pallas_call | solution.py:286
  54.8 3.0 %copy.7 = f32[1,30,128,128]{3,2,1,0:T(8,128)} copy(f32[1,30,128,128]{3,2,1,0:T(8,128)} %bitcast.2) | data formatting | bytes 3932160
